TPU v7x, 32 devices: a whole 2x2x4 slice. The times are simulated.
32 devices in a mesh: rep: 1, ep: 32 (over z, y, x, core).
Axes of the slice: x: 2, y: 2, z: 4, core: 2. Of those that a mesh axis runs over, the one named last changes fastest.
Arguments:
- kv_cache: bfloat16 [128, 256, 576], P(('rep', 'ep')), may hold values from -6 to 6
- cache_len: int32 [128], P('rep'), may hold values from 1 to 254, 16384 in all
- move_slot: int32 [32, 2], P('rep'), may hold values from 0 to 3, as said below
- move_key: int32 [2], P('rep'), may hold values from 1 to 31
- queries: bfloat16 [2, 128, 128, 576], P(None, ('rep', 'ep')), may hold values from -150 to 150
- new_latent: bfloat16 [2, 128, 576], P(None, ('rep', 'ep')), may hold values from -6 to 6
- moe_in: bfloat16 [2, 128, 7168], P(None, ('rep', 'ep')), may hold values from -6 to 6
- expert_ids: int32 [2, 128, 1], P(None, ('rep', 'ep')), may hold values from 0 to 1; in each aligned block of 4 rows (0 to 3, 4 to 7, ..., all dimensions but the last counted through in order) at most 3 rows name the same one
- expert_weights: float32 [2, 128, 1], P(None, ('rep', 'ep')), may hold values from 0.25 to 1
- w_gate: bfloat16 [7168, 4096], P(None, 'ep'), may hold values from -0.0625 to 0.0625
- w_up: bfloat16 [7168, 4096], P(None, 'ep'), may hold values from -0.0625 to 0.0625
- w_down: bfloat16 [4096, 7168], P('ep'), may hold values from -0.125 to 0.125
Outputs:
- attention_out: bfloat16 [2, 128, 128, 512], P(None, ('rep', 'ep'))
- cache_out: bfloat16 [128, 256, 576], P(('rep', 'ep'))
- moe_out: bfloat16 [2, 128, 7168], P(None, ('rep', 'ep'))
Inputs may be any that keep to these rules, and one draw needn't show every extreme that they name: `expert_ids`: in each step, no device routes more than 3 of its tokens to one expert; each token names different experts. `cache_len`: each request slot has at least one cached position; positions at and beyond its length are not part of it. `move_slot`: each row names 2 different slots. Move k pairs device i with device i XOR move_key[k].
All inputs are finite; a program needn't handle non-finite values.
Results may differ from a plain program's by a relative error of at most 0.0085.
Values may be sent and summed in bfloat16 or wider, within the bound.
A program may use at most 128 MiB of HBM per device.

v0:
```python
import functools

import jax
import jax.numpy as jnp
from jax import lax
from jax.experimental import pallas as pl
from jax.experimental.pallas import tpu as pltpu
from jax.sharding import PartitionSpec as P

LAT = 512
SPLIT = 16
MESH = pl.DeviceIdType.MESH
LANES = 128
ORDERS = ((3, 1, 2), (3, 2, 1), (3, 1, 2), (3, 2, 1))

softmax_scale = 192.0 ** (-0.5)


def flipped(index, distance):
    return index + distance * (1 - 2 * ((index // distance) % 2))


def flip_all(index, mask):
    distance = 1
    while distance <= mask:
        if mask & distance:
            index = flipped(index, distance)
        distance *= 2
    return index


def part_columns(width):
    tiles, count = width // LANES, len(ORDERS)
    edges = [tiles * p // count * LANES for p in range(count + 1)]
    return [(edges[p], edges[p + 1] - edges[p]) for p in range(count)]


def slot_of(part, mask):
    slot = 8 if mask & 1 else 0
    for place, bit in enumerate(ORDERS[part]):
        if mask >> bit & 1:
            slot |= 1 << place
    return slot


def layer_kernel(groups, columns, orders, *refs):
    slot_ref, key_ref, id_ref, weight_ref, kv_ref, tok_ref, wg_ref, wu_ref, wd_ref = refs[:9]
    out_ref, arr_ref, outgoing, landed = refs[9:13]
    scratch = refs[13:]
    parts = len(columns)
    wgu, wd = scratch[:2]
    arrive = scratch[2 : 2 + parts]
    held = scratch[2 + parts : 2 + 2 * parts]
    sums = scratch[2 + 2 * parts : 2 + 3 * parts]
    taken = scratch[2 + 3 * parts : 2 + 4 * parts]
    final = scratch[2 + 4 * parts : 2 + 5 * parts]
    ended = scratch[2 + 5 * parts : 2 + 6 * parts]
    load_sem, send_sem, recv_sem = scratch[2 + 6 * parts :]
    me = lax.axis_index("ep")
    token_rows = tok_ref.shape[0]
    rows = groups * token_rows
    half = wg_ref.shape[1]

    loads = [
        pltpu.make_async_copy(wg_ref, wgu.at[:, 0:half], load_sem.at[0]),
        pltpu.make_async_copy(wu_ref, wgu.at[:, half : 2 * half], load_sem.at[1]),
        pltpu.make_async_copy(wd_ref, wd, load_sem.at[2]),
    ]
    for load in loads:
        load.start()

    partners = [1, 2, 4, 8] + [SPLIT * d for d in range(1, groups)]
    barrier = pltpu.get_barrier_semaphore()
    for mask in partners:
        pl.semaphore_signal(
            barrier, inc=1, device_id={"ep": flip_all(me, mask)}, device_id_type=MESH
        )
    pl.semaphore_wait(barrier, len(partners))

    counter = [0]

    def send(source, target, mask):
        number = counter[0]
        counter[0] += 1
        copy = pltpu.make_async_remote_copy(
            src_ref=source,
            dst_ref=target,
            send_sem=send_sem.at[number],
            recv_sem=recv_sem.at[number],
            device_id={"ep": flip_all(me, mask)},
            device_id_type=MESH,
        )
        copy.start()
        return copy

    everything = []

    moves, chunk = outgoing.shape[0], outgoing.shape[1] // len(orders)
    moving = [None] * len(orders)
    stage_of = [0] * len(orders)

    def part_of(c):
        return slice(c * chunk, (c + 1) * chunk)

    def depart(c):
        stage = stage_of[c]
        source = outgoing if stage == 0 else landed.at[stage - 1]
        moving[c] = send(
            source.at[:, part_of(c)], landed.at[stage, :, part_of(c)], 1 << orders[c][stage]
        )
        everything.append(moving[c])

    def advance():
        for c in range(len(orders)):
            moving[c].wait_recv()
            stage = stage_of[c]
            final_stage = stage == len(orders[c]) - 1
            for k in range(moves):
                other = landed[stage, k, part_of(c)]
                own = outgoing[k, part_of(c)] if stage == 0 else landed[stage - 1, k, part_of(c)]
                bit = (key_ref[k] // (1 << orders[c][stage])) % 2
                chosen = jnp.where(bit == 1, other, own)
                if final_stage:
                    arr_ref[k, part_of(c)] = chosen
                else:
                    landed[stage, k, part_of(c)] = chosen
            stage_of[c] += 1
            if not final_stage:
                depart(c)

    first = []
    for p, (start, width) in enumerate(columns):
        first.append(
            [
                send(tok_ref.at[:, start : start + width], arrive[p].at[d], SPLIT * d)
                for d in range(1, groups)
            ]
        )

    for k in range(moves):
        slot = slot_ref[me * moves + k]
        payload = kv_ref[0]
        for r in range(1, kv_ref.shape[0]):
            payload = jnp.where(slot == r, kv_ref[r], payload)
        outgoing[k] = payload
    for c in range(len(orders)):
        depart(c)

    across = [[] for _ in range(parts)]
    link = [None] * parts
    for p, (start, width) in enumerate(columns):
        for copy in first[p]:
            copy.wait_recv()
        pieces = [tok_ref[:, start : start + width].astype(jnp.float32)]
        pieces += [arrive[p][d].astype(jnp.float32) for d in range(1, groups)]
        held[p][0] = jnp.concatenate(pieces, axis=0).astype(jnp.bfloat16)
        link[p] = send(held[p].at[0:1], held[p].at[1:2], 1 << ORDERS[p][0])
        across[p].append(send(held[p].at[0:1], held[p].at[8:9], 1))
        everything += first[p]
    for stage in range(3):
        have = 1 << stage
        for p in range(parts):
            link[p].wait_recv()
            everything.append(link[p])
            if stage < 2:
                link[p] = send(
                    held[p].at[0 : 2 * have],
                    held[p].at[2 * have : 4 * have],
                    1 << ORDERS[p][stage + 1],
                )
            across[p].append(
                send(held[p].at[have : 2 * have], held[p].at[8 + have : 8 + 2 * have], 1)
            )
        if stage == 0:
            advance()

    loads[0].wait()
    loads[1].wait()
    act = None
    for p, (start, width) in enumerate(columns):
        for copy in across[p]:
            copy.wait_recv()
        everything += across[p]
        product = jnp.dot(
            held[p][...].reshape(SPLIT * rows, width),
            wgu[start : start + width, :],
            preferred_element_type=jnp.float32,
        )
        ordered = [None] * SPLIT
        for mask in range(SPLIT):
            slot = slot_of(p, mask)
            ordered[mask] = product[slot * rows : (slot + 1) * rows]
        product = jnp.concatenate(ordered, axis=0)
        act = product if act is None else act + product
    gate, up = act[:, 0:half], act[:, half : 2 * half]
    hidden = (gate / (1.0 + jnp.exp(-gate)) * up)
    loads[2].wait()

    across = [[] for _ in range(parts)]
    for p, (start, width) in enumerate(columns):
        ordered = [None] * SPLIT
        for mask in range(SPLIT):
            ordered[slot_of(p, mask)] = hidden[mask * rows : (mask + 1) * rows]
        mine = jnp.concatenate(ordered, axis=0).astype(jnp.bfloat16)
        down = wd[:, start : start + width]
        for low in (8, 0):
            sums[p][low : low + 8] = (
                jnp.dot(
                    mine[low * rows : (low + 8) * rows], down, preferred_element_type=jnp.float32
                )
                .astype(jnp.bfloat16)
                .reshape(8, rows, width)
            )
            if low:
                for a, b in ((12, 16), (10, 12), (8, 10)):
                    across[p].append(send(sums[p].at[a:b], taken[p].at[a:b], 1))

    def add(p, low, high, shift):
        total = sums[p][low:high].astype(jnp.float32)
        total += taken[p][low + shift : high + shift].astype(jnp.float32)
        sums[p][low:high] = total.astype(jnp.bfloat16)

    for p in range(parts):
        across[p][0].wait_recv()
        add(p, 4, 8, 8)
        link[p] = send(sums[p].at[4:8], taken[p].at[4:8], 1 << ORDERS[p][2])
    for p in range(parts):
        across[p][1].wait_recv()
        across[p][2].wait_recv()
        everything += across[p]
        add(p, 0, 4, 8)
    advance()
    for stage in (1, 0):
        have = 1 << stage
        for p in range(parts):
            link[p].wait_recv()
            everything.append(link[p])
            add(p, have, 2 * have, 2 * have)
            link[p] = send(
                sums[p].at[have : 2 * have], taken[p].at[have : 2 * have], 1 << ORDERS[p][stage]
            )
        for p in range(parts):
            add(p, 0, have, 2 * have)
        if stage == 1:
            advance()

    last = []
    for p in range(parts):
        link[p].wait_recv()
        everything.append(link[p])
        total = sums[p][0].astype(jnp.float32) + taken[p][1].astype(jnp.float32)
        for d in range(groups):
            final[p][d] = total[d * token_rows : (d + 1) * token_rows].astype(jnp.bfloat16)
        last.append(
            [send(final[p].at[d], ended[p].at[d], SPLIT * d) for d in range(1, groups)]
        )
    advance()
    tops = id_ref.shape[0] // token_rows
    row_of = lax.broadcasted_iota(jnp.int32, (token_rows, LANES), 0)
    gains = []
    for d in range(groups):
        expert = flip_all(me, SPLIT * d) // SPLIT
        gain = jnp.zeros((token_rows, LANES), jnp.float32)
        for row in range(token_rows):
            for top in range(tops):
                at = row * tops + top
                taken_here = jnp.where(id_ref[at] == expert, weight_ref[at], jnp.float32(0.0))
                gain = gain + jnp.where(row_of == row, taken_here, jnp.float32(0.0))
        gains.append(gain[:, 0:1])
    for p, (start, width) in enumerate(columns):
        mixed = gains[0] * final[p][0].astype(jnp.float32)
        for d in range(1, groups):
            last[p][d - 1].wait_recv()
            mixed += gains[d] * ended[p][d].astype(jnp.float32)
        out_ref[:, start : start + width] = mixed.astype(jnp.bfloat16)
        everything += last[p]
    while stage_of[0] < len(orders[0]):
        advance()
    for copy in everything:
        copy.wait_send()


def layer(slots_flat, move_key, kv, moe_in, expert_ids, expert_weights, w_gate, w_up, w_down):
    steps, token_count, width = moe_in.shape
    devices = lax.axis_size("ep")
    groups = devices // SPLIT
    rows = steps * token_count
    tokens = moe_in.reshape(rows, width)
    columns = part_columns(width)
    hidden = w_gate.shape[1]
    slot_rows = groups * rows
    moves = move_key.shape[0]
    high = list(range(4, devices.bit_length() - 1))
    orders = ([1] + high + [3, 2, 0], [2, 3] + high + [1, 0])
    bf16 = jnp.bfloat16
    payload = (moves,) + kv.shape[1:]
    scratch = [pltpu.VMEM(payload, bf16), pltpu.VMEM((len(orders[0]),) + payload, bf16)]
    scratch += [pltpu.VMEM((width, 2 * hidden), bf16), pltpu.VMEM((hidden, width), bf16)]
    outer, inner = (groups, rows), (SPLIT, slot_rows)
    for shape in (outer, inner, inner, inner, outer, outer):
        scratch += [pltpu.VMEM(shape + (wide,), bf16) for _, wide in columns]
    copies = len(columns) * (2 * (groups - 1) + 13) + len(orders) * len(orders[0])
    scratch += [pltpu.SemaphoreType.DMA((3,))] + [pltpu.SemaphoreType.DMA((copies,))] * 2
    vmem, anywhere = pl.BlockSpec(memory_space=pltpu.VMEM), pl.BlockSpec(memory_space=pl.ANY)
    smem = pl.BlockSpec(memory_space=pltpu.SMEM)
    out, arrivals = pl.pallas_call(
        functools.partial(layer_kernel, groups, columns, orders),
        out_shape=[
            jax.ShapeDtypeStruct((rows, width), bf16),
            jax.ShapeDtypeStruct(payload, bf16),
        ],
        in_specs=[smem] * 4 + [vmem, vmem, anywhere, anywhere, anywhere],
        out_specs=[vmem, vmem],
        scratch_shapes=scratch,
        compiler_params=pltpu.CompilerParams(
            collective_id=0, has_side_effects=True, vmem_limit_bytes=60 * 2**20
        ),
        name="layer",
    )(
        slots_flat,
        move_key,
        expert_ids.reshape(-1),
        expert_weights.reshape(-1),
        kv,
        tokens,
        w_gate,
        w_up,
        w_down,
    )
    return out.reshape(steps, token_count, width), arrivals


def attend_kernel(
    me_ref, slot_ref, key_ref, len_ref, kv_ref, arr_ref, q_ref, new_ref, out_ref, cache_ref
):
    r = pl.program_id(0)
    me, slots, moves = me_ref[0], pl.num_programs(0), arr_ref.shape[0]
    length = len_ref[me * slots + r]
    rows = kv_ref[0]
    for k in range(moves):
        here = slot_ref[me * moves + k] == r
        partner = me ^ key_ref[k]
        length = jnp.where(here, len_ref[partner * slots + slot_ref[partner * moves + k]], length)
        rows = jnp.where(here, arr_ref[k], rows)
    steps, heads = q_ref.shape[0], q_ref.shape[3]
    positions = rows.shape[1]
    step_of = lax.broadcasted_iota(jnp.int32, (steps, positions), 0)
    place = lax.broadcasted_iota(jnp.int32, (steps, positions), 1)
    spread = jnp.where(place == length + step_of, 1.0, 0.0).astype(jnp.bfloat16)
    fresh = lax.dot_general(
        new_ref[0], spread, (((0,), (0,)), ((), ())), preferred_element_type=jnp.float32
    )
    column = lax.broadcasted_iota(jnp.int32, rows.shape, 1)
    is_new = (column >= length) & (column < length + steps)
    rows = jnp.where(is_new, fresh, rows.astype(jnp.float32)).astype(jnp.bfloat16)
    cache_ref[0] = rows
    merged = jnp.concatenate([q_ref[s, 0] for s in range(steps)], axis=1)
    scores = (
        lax.dot_general(merged, rows, (((0,), (0,)), ((), ())), preferred_element_type=jnp.float32)
        * softmax_scale
    )
    at = lax.broadcasted_iota(jnp.int32, scores.shape, 1)
    step = lax.broadcasted_iota(jnp.int32, scores.shape, 0) // heads
    scores = jnp.where(at < length + step + 1, scores, jnp.float32(-1e30))
    weights = jnp.exp(scores - jnp.max(scores, axis=-1, keepdims=True))
    probabilities = (weights / jnp.sum(weights, axis=-1, keepdims=True)).astype(jnp.bfloat16)
    attended = lax.dot_general(
        probabilities, rows[:LAT], (((1,), (1,)), ((), ())), preferred_element_type=jnp.float32
    ).astype(jnp.bfloat16)
    for s in range(steps):
        out_ref[s, 0] = attended[s * heads : (s + 1) * heads]


def attend(me, slots_flat, move_key, cache_len, kv, arrivals, queries, new_latent):
    slots, width, positions = kv.shape
    steps, _, _, heads = queries.shape
    moves = arrivals.shape[0]
    grid = pltpu.PrefetchScalarGridSpec(
        num_scalar_prefetch=4,
        grid=(slots,),
        in_specs=[
            pl.BlockSpec((1, width, positions), lambda r, *_: (r, 0, 0)),
            pl.BlockSpec((moves, width, positions), lambda r, *_: (0, 0, 0)),
            pl.BlockSpec((steps, 1, width, heads), lambda r, *_: (0, r, 0, 0)),
            pl.BlockSpec((1, steps, width), lambda r, *_: (r, 0, 0)),
        ],
        out_specs=[
            pl.BlockSpec((steps, 1, heads, LAT), lambda r, *_: (0, r, 0, 0)),
            pl.BlockSpec((1, width, positions), lambda r, *_: (r, 0, 0)),
        ],
    )
    return pl.pallas_call(
        attend_kernel,
        grid_spec=grid,
        out_shape=[
            jax.ShapeDtypeStruct((steps, slots, heads, LAT), jnp.bfloat16),
            jax.ShapeDtypeStruct(kv.shape, jnp.bfloat16),
        ],
        compiler_params=pltpu.CompilerParams(vmem_limit_bytes=60 * 2**20),
        name="attend",
    )(
        me,
        slots_flat,
        move_key,
        cache_len,
        kv,
        arrivals,
        queries,
        jnp.transpose(new_latent, (1, 0, 2)),
    )


def body(
    kv_cache,
    cache_len,
    move_slot,
    move_key,
    queries,
    new_latent,
    moe_in,
    expert_ids,
    expert_weights,
    w_gate,
    w_up,
    w_down,
):
    me = lax.axis_index("ep").reshape(1)
    slots_flat = move_slot.reshape(-1)
    kv = jnp.transpose(kv_cache, (0, 2, 1))
    moe_out, arrivals = layer(
        slots_flat, move_key, kv, moe_in, expert_ids, expert_weights, w_gate, w_up, w_down
    )
    attention_out, cache = attend(
        me,
        slots_flat,
        move_key,
        cache_len,
        kv,
        arrivals,
        jnp.transpose(queries, (0, 1, 3, 2)),
        new_latent,
    )
    return (attention_out, jnp.transpose(cache, (0, 2, 1)), moe_out)


def solution(mesh):
    in_specs = (
        P(("rep", "ep"), None, None),
        P("rep"),
        P("rep", None),
        P("rep"),
        P(None, ("rep", "ep"), None, None),
        P(None, ("rep", "ep"), None),
        P(None, ("rep", "ep"), None),
        P(None, ("rep", "ep"), None),
        P(None, ("rep", "ep"), None),
        P(None, "ep"),
        P(None, "ep"),
        P("ep", None),
    )
    out_specs = (
        P(None, ("rep", "ep"), None, None),
        P(("rep", "ep"), None, None),
        P(None, ("rep", "ep"), None),
    )
    return jax.shard_map(body, mesh=mesh, in_specs=in_specs, out_specs=out_specs, check_vma=False)
```

profile of v0, /device:TPU:1, one launch (start us, length us, event | category | flops | bytes accessed | tf_op | source)
XLA Modules:
  0.0 84.1 jit_solution(6516979003113095904)
XLA Ops:
  0.6 0.5 broadcast.6
  1.1 1.3 %reduce.6 = s32[2,4]{1,0:T(2,128)S(1)} reduce(s32[2,4,1]{1,2,0:T(1,128)} %param.19, s32[]{:T(128)} %broadcast.6), dimensions={2}, to_apply=%param.19.reduce_sub_computation.3 | reduce | bytes 68 | tf_op args[7]
  2.5 0.6 reshape.26.refs_2_
  3.1 0.5 broadcast.7
  3.6 1.3 %reduce.7 = f32[2,4]{1,0:T(2,128)S(1)} reduce(f32[2,4,1]{1,2,0:T(1,128)} %param.20, f32[]{:T(128)} %broadcast.7), dimensions={2}, to_apply=%param.20.reduce_sub_computation.3 | reduce | bytes 68 | tf_op args[8]
  4.9 0.6 reshape.27.refs_3_
  5.5 1.3 %copy.20 = bf16[2,4,576]{2,0,1:T(2,128)(2,1)} copy(bf16[2,4,576]{2,1,0:T(4,128)(2,1)} %param.17) | data formatting | bytes 18432 | tf_op args[5]
  6.8 0.8 copy.17
  7.6 0.6 reshape.25.refs_0_.slot_ref
  8.2 1.6 %reshape.28.refs_5_ = bf16[8,7168]{1,0:T(8,128)(2,1)} reshape(bf16[2,4,7168]{2,1,0:T(4,128)(2,1)} %param.18) | data formatting | bytes 229376 | tf_op jit(solution)/shard_map/reshape | solution.py:288
  9.8 65.7 %layer.1 = (bf16[8,7168]{1,0:T(8,128)(2,1)}, bf16[2,576,256]{2,1,0:T(8,128)(2,1)}) custom-call(s32[64]{0:T(128)} %reshape.25.refs_0_.slot_ref, s32[2]{0:T(128)} %key_ref.1, s32[8]{0:T(128)} %reshape.26.refs_2_, f32[8]{0:T(128)} %reshape.27.refs_3_, bf16[4,576,256]{2,1,0:T(8,128)(2,1)} %bitcast.9, bf16[8,7168]{1,0:T(8,128)(2,1)} %reshape.28.refs_5_, ...), custom_call_target="tpu_custom_call" | custom-call | tf_op jit(solution)/shard_map/layer/pallas_call | solution.py:306
  75.5 1.6 %reshape.29 = bf16[2,4,7168]{2,1,0:T(4,128)(2,1)} reshape(bf16[8,7168]{1,0:T(8,128)(2,1)} %get-tuple-element.10) | data formatting | bytes 229376 | tf_op jit(solution)/shard_map/reshape | solution.py:330
  77.1 7.0 %attend.1 = (bf16[2,4,128,512]{3,2,1,0:T(8,128)(2,1)}, bf16[4,576,256]{2,1,0:T(8,128)(2,1)}) custom-call(s32[1]{0:T(128)} %bitcast.me_ref, s32[64]{0:T(128)} %reshape.25.refs_0_.slot_ref, s32[2]{0:T(128)} %key_ref.1, s32[128]{0:T(128)} %len_ref.1, bf16[4,576,256]{2,1,0:T(8,128)(2,1)} %bitcast.10, bf16[2,576,256]{2,1,0:T(8,128)(2,1)} %get-tuple-element.7.arr_ref, ...), custom_call_target="tpu_custom_call" | custom-call | tf_op jit(solution)/shard_map/attend/pallas_call | solution.py:392
where the time goes:
time: 84.5 us; the launch traced here: 84.1 us
  Pallas kernels  72.7 us (86%)
  local copies, waits for them, and re-layouts  8.08 us (10%)
  other arithmetic  2.68 us (3%)
    pallas_call x1, Pallas kernels, layer(): pl.pallas_call(functools.partial(layer_kernel, groups, columns, orders),...  65.7 us
    pallas_call x1, Pallas kernels, attend(): pl.pallas_call(attend_kernel, grid_spec=grid, out_shape=[jax.ShapeDtypeSt...  7 us
    unnamed x4, local copies, waits for them, and re-layouts  3.1 us
    unnamed x2, other arithmetic  2.68 us

commit v1 on v0

--- a/solution.py
+++ b/solution.py
@@ -11,7 +11,7 @@
 SPLIT = 16
 MESH = pl.DeviceIdType.MESH
 LANES = 128
-ORDERS = ((3, 1, 2), (3, 2, 1), (3, 1, 2), (3, 2, 1))
+ORDERS = ((3, 1, 2), (3, 2, 1)) * 3
 
 softmax_scale = 192.0 ** (-0.5)
 
@@ -29,10 +29,12 @@
     return index
 
 
-def part_columns(width):
-    tiles, count = width // LANES, len(ORDERS)
-    edges = [tiles * p // count * LANES for p in range(count + 1)]
-    return [(edges[p], edges[p + 1] - edges[p]) for p in range(count)]
+def part_columns(width, tokens):
+    wide, cuts = width // tokens, len(ORDERS) // (tokens - 1)
+    edges = [wide // LANES * p // cuts * LANES for p in range(cuts + 1)]
+    return [
+        (section, edges[p], edges[p + 1] - edges[p]) for section in range(tokens - 1) for p in range(cuts)
+    ]
 
 
 def slot_of(part, mask):
@@ -49,15 +51,13 @@
     scratch = refs[13:]
     parts = len(columns)
     wgu, wd = scratch[:2]
-    arrive = scratch[2 : 2 + parts]
-    held = scratch[2 + parts : 2 + 2 * parts]
-    sums = scratch[2 + 2 * parts : 2 + 3 * parts]
-    taken = scratch[2 + 3 * parts : 2 + 4 * parts]
-    final = scratch[2 + 4 * parts : 2 + 5 * parts]
-    ended = scratch[2 + 5 * parts : 2 + 6 * parts]
-    load_sem, send_sem, recv_sem = scratch[2 + 6 * parts :]
+    packed, arrive, held, sums, taken, final, ended = [
+        scratch[2 + n * parts : 2 + (n + 1) * parts] for n in range(7)
+    ]
+    load_sem, send_sem, recv_sem = scratch[2 + 7 * parts :]
     me = lax.axis_index("ep")
-    token_rows = tok_ref.shape[0]
+    steps, per_step, width = tok_ref.shape
+    token_rows, tail = steps * per_step, width // per_step * (per_step - 1)
     rows = groups * token_rows
     half = wg_ref.shape[1]
 
@@ -128,17 +128,61 @@
             if not final_stage:
                 depart(c)
 
+    rank, gain = [], []
+    for d in range(groups):
+        expert = flip_all(me, SPLIT * d) // SPLIT
+        rank.append([])
+        gain.append([])
+        for s in range(steps):
+            seen = 0
+            for t in range(per_step):
+                named, weight = 0, jnp.float32(0.0)
+                for top in range(id_ref.shape[1]):
+                    match = id_ref[s, top, t] == expert
+                    named = named + jnp.where(match, 1, 0)
+                    weight = weight + jnp.where(match, weight_ref[s, top, t], jnp.float32(0.0))
+                rank[d].append(jnp.where(named > 0, seen, -1))
+                gain[d].append(weight)
+                seen = seen + named
+
+    def chosen_rows(d, section, transposed):
+        shape = (token_rows, token_rows)
+        packed_row = lax.broadcasted_iota(jnp.int32, shape, 1 if transposed else 0)
+        token_row = lax.broadcasted_iota(jnp.int32, shape, 0 if transposed else 1)
+        main = jnp.zeros(shape, jnp.float32)
+        last = jnp.zeros(shape, jnp.float32)
+        for row in range(token_rows):
+            base = row // per_step * per_step
+            place = rank[d][row]
+            at_main = jnp.where(place >= 0, base + place, -1)
+            at_last = jnp.where(place == section, base + per_step - 1, -1)
+            main += jnp.where((token_row == row) & (packed_row == at_main), 1.0, 0.0)
+            last += jnp.where((token_row == row) & (packed_row == at_last), 1.0, 0.0)
+        return main, last
+
+    tokens = jnp.concatenate([tok_ref[s].astype(jnp.float32) for s in range(steps)], axis=0)
+
+    def pack(d, section, start, low, wide):
+        main, last = chosen_rows(d, section, False)
+        matrix = jnp.concatenate([main, last], axis=1).astype(jnp.bfloat16)
+        both = jnp.concatenate(
+            [tokens[:, start : start + wide], tokens[:, low : low + wide]], axis=0
+        ).astype(jnp.bfloat16)
+        return jnp.dot(matrix, both, preferred_element_type=jnp.float32)
+
+    place_of = []
+    for section, offset, wide in columns:
+        place_of.append((section, section * (width // per_step) + offset, tail + offset, wide))
+
     first = []
-    for p, (start, width) in enumerate(columns):
-        first.append(
-            [
-                send(tok_ref.at[:, start : start + width], arrive[p].at[d], SPLIT * d)
-                for d in range(1, groups)
-            ]
-        )
+    for p, place in enumerate(place_of):
+        first.append([])
+        for d in range(1, groups):
+            packed[p][d] = pack(d, *place).astype(jnp.bfloat16)
+            first[p].append(send(packed[p].at[d], arrive[p].at[d], SPLIT * d))
 
     for k in range(moves):
-        slot = slot_ref[me * moves + k]
+        slot = slot_ref[k, me]
         payload = kv_ref[0]
         for r in range(1, kv_ref.shape[0]):
             payload = jnp.where(slot == r, kv_ref[r], payload)
@@ -148,10 +192,11 @@
 
     across = [[] for _ in range(parts)]
     link = [None] * parts
-    for p, (start, width) in enumerate(columns):
+    for p, place in enumerate(place_of):
+        mine = pack(0, *place)
         for copy in first[p]:
             copy.wait_recv()
-        pieces = [tok_ref[:, start : start + width].astype(jnp.float32)]
+        pieces = [mine]
         pieces += [arrive[p][d].astype(jnp.float32) for d in range(1, groups)]
         held[p][0] = jnp.concatenate(pieces, axis=0).astype(jnp.bfloat16)
         link[p] = send(held[p].at[0:1], held[p].at[1:2], 1 << ORDERS[p][0])
@@ -177,15 +222,17 @@
     loads[0].wait()
     loads[1].wait()
     act = None
-    for p, (start, width) in enumerate(columns):
+    in_step = lax.broadcasted_iota(jnp.int32, (SPLIT * rows, 2 * half), 0) % per_step
+    for p, (section, start, low, wide) in enumerate(place_of):
         for copy in across[p]:
             copy.wait_recv()
         everything += across[p]
-        product = jnp.dot(
-            held[p][...].reshape(SPLIT * rows, width),
-            wgu[start : start + width, :],
-            preferred_element_type=jnp.float32,
-        )
+        block = held[p][...].reshape(SPLIT * rows, wide)
+        product = jnp.dot(block, wgu[start : start + wide, :], preferred_element_type=jnp.float32)
+        ends = jnp.dot(block, wgu[low : low + wide, :], preferred_element_type=jnp.float32)
+        shift = per_step - 1 - section
+        ends = jnp.concatenate([ends[shift:], ends[:shift]], axis=0)
+        product += jnp.where(in_step == section, ends, 0.0)
         ordered = [None] * SPLIT
         for mask in range(SPLIT):
             slot = slot_of(p, mask)
@@ -197,19 +244,25 @@
     loads[2].wait()
 
     across = [[] for _ in range(parts)]
-    for p, (start, width) in enumerate(columns):
+    in_step = in_step[:, 0:half]
+    hidden = jnp.where(in_step == per_step - 1, 0.0, hidden)
+    for p, (section, start, low, wide) in enumerate(place_of):
+        shift = per_step - 1 - section
+        moved = jnp.concatenate([hidden[-shift:], hidden[:-shift]], axis=0)
+        moved = jnp.where(in_step == per_step - 1, moved, 0.0)
+        both = jnp.concatenate([hidden, moved], axis=1)
         ordered = [None] * SPLIT
         for mask in range(SPLIT):
-            ordered[slot_of(p, mask)] = hidden[mask * rows : (mask + 1) * rows]
+            ordered[slot_of(p, mask)] = both[mask * rows : (mask + 1) * rows]
         mine = jnp.concatenate(ordered, axis=0).astype(jnp.bfloat16)
-        down = wd[:, start : start + width]
+        down = jnp.concatenate([wd[:, start : start + wide], wd[:, low : low + wide]], axis=0)
         for low in (8, 0):
             sums[p][low : low + 8] = (
                 jnp.dot(
                     mine[low * rows : (low + 8) * rows], down, preferred_element_type=jnp.float32
                 )
                 .astype(jnp.bfloat16)
-                .reshape(8, rows, width)
+                .reshape(8, rows, wide)
             )
             if low:
                 for a, b in ((12, 16), (10, 12), (8, 10)):
@@ -255,38 +308,49 @@
             [send(final[p].at[d], ended[p].at[d], SPLIT * d) for d in range(1, groups)]
         )
     advance()
-    tops = id_ref.shape[0] // token_rows
     row_of = lax.broadcasted_iota(jnp.int32, (token_rows, LANES), 0)
     gains = []
     for d in range(groups):
-        expert = flip_all(me, SPLIT * d) // SPLIT
-        gain = jnp.zeros((token_rows, LANES), jnp.float32)
+        column = jnp.zeros((token_rows, LANES), jnp.float32)
         for row in range(token_rows):
-            for top in range(tops):
-                at = row * tops + top
-                taken_here = jnp.where(id_ref[at] == expert, weight_ref[at], jnp.float32(0.0))
-                gain = gain + jnp.where(row_of == row, taken_here, jnp.float32(0.0))
-        gains.append(gain[:, 0:1])
-    for p, (start, width) in enumerate(columns):
-        mixed = gains[0] * final[p][0].astype(jnp.float32)
-        for d in range(1, groups):
-            last[p][d - 1].wait_recv()
-            mixed += gains[d] * ended[p][d].astype(jnp.float32)
-        out_ref[:, start : start + width] = mixed.astype(jnp.bfloat16)
+            column += jnp.where(row_of == row, gain[d][row], jnp.float32(0.0))
+        gains.append(column[:, 0:1])
+    ends = {}
+    for p, (section, start, low, wide) in enumerate(place_of):
+        mixed = None
+        for d in range(groups):
+            if d:
+                last[p][d - 1].wait_recv()
+            home = ended[p][d] if d else final[p][0]
+            main, tails = chosen_rows(d, section, True)
+            matrix = jnp.concatenate([main, tails], axis=0).astype(jnp.bfloat16)
+            unpacked = jnp.dot(matrix, home, preferred_element_type=jnp.float32)
+            unpacked = unpacked * jnp.concatenate([gains[d], gains[d]], axis=0)
+            mixed = unpacked if mixed is None else mixed + unpacked
+        for s in range(steps):
+            out_ref[s, :, start : start + wide] = mixed[
+                s * per_step : (s + 1) * per_step
+            ].astype(jnp.bfloat16)
+        after = mixed[token_rows:]
+        ends[low] = (ends[low][0] + after, wide) if low in ends else (after, wide)
         everything += last[p]
+    for low, (mixed, wide) in ends.items():
+        for s in range(steps):
+            out_ref[s, :, low : low + wide] = mixed[s * per_step : (s + 1) * per_step].astype(
+                jnp.bfloat16
+            )
     while stage_of[0] < len(orders[0]):
         advance()
     for copy in everything:
         copy.wait_send()
 
 
-def layer(slots_flat, move_key, kv, moe_in, expert_ids, expert_weights, w_gate, w_up, w_down):
+def layer(slot_table, move_key, kv, moe_in, expert_ids, expert_weights, w_gate, w_up, w_down):
     steps, token_count, width = moe_in.shape
     devices = lax.axis_size("ep")
     groups = devices // SPLIT
     rows = steps * token_count
-    tokens = moe_in.reshape(rows, width)
-    columns = part_columns(width)
+    columns = part_columns(width, token_count)
     hidden = w_gate.shape[1]
     slot_rows = groups * rows
     moves = move_key.shape[0]
@@ -297,8 +361,8 @@
     scratch = [pltpu.VMEM(payload, bf16), pltpu.VMEM((len(orders[0]),) + payload, bf16)]
     scratch += [pltpu.VMEM((width, 2 * hidden), bf16), pltpu.VMEM((hidden, width), bf16)]
     outer, inner = (groups, rows), (SPLIT, slot_rows)
-    for shape in (outer, inner, inner, inner, outer, outer):
-        scratch += [pltpu.VMEM(shape + (wide,), bf16) for _, wide in columns]
+    for shape in (outer, outer, inner, inner, inner, outer, outer):
+        scratch += [pltpu.VMEM(shape + (wide,), bf16) for _, _, wide in columns]
     copies = len(columns) * (2 * (groups - 1) + 13) + len(orders) * len(orders[0])
     scratch += [pltpu.SemaphoreType.DMA((3,))] + [pltpu.SemaphoreType.DMA((copies,))] * 2
     vmem, anywhere = pl.BlockSpec(memory_space=pltpu.VMEM), pl.BlockSpec(memory_space=pl.ANY)
@@ -306,7 +370,7 @@
     out, arrivals = pl.pallas_call(
         functools.partial(layer_kernel, groups, columns, orders),
         out_shape=[
-            jax.ShapeDtypeStruct((rows, width), bf16),
+            jax.ShapeDtypeStruct(moe_in.shape, bf16),
             jax.ShapeDtypeStruct(payload, bf16),
         ],
         in_specs=[smem] * 4 + [vmem, vmem, anywhere, anywhere, anywhere],
@@ -317,17 +381,17 @@
         ),
         name="layer",
     )(
-        slots_flat,
+        slot_table,
         move_key,
-        expert_ids.reshape(-1),
-        expert_weights.reshape(-1),
+        jnp.transpose(expert_ids, (0, 2, 1)),
+        jnp.transpose(expert_weights, (0, 2, 1)),
         kv,
-        tokens,
+        moe_in,
         w_gate,
         w_up,
         w_down,
     )
-    return out.reshape(steps, token_count, width), arrivals
+    return out, arrivals
 
 
 def attend_kernel(
@@ -338,18 +402,21 @@
     length = len_ref[me * slots + r]
     rows = kv_ref[0]
     for k in range(moves):
-        here = slot_ref[me * moves + k] == r
+        here = slot_ref[k, me] == r
         partner = me ^ key_ref[k]
-        length = jnp.where(here, len_ref[partner * slots + slot_ref[partner * moves + k]], length)
+        length = jnp.where(here, len_ref[partner * slots + slot_ref[k, partner]], length)
         rows = jnp.where(here, arr_ref[k], rows)
     steps, heads = q_ref.shape[0], q_ref.shape[3]
     positions = rows.shape[1]
-    step_of = lax.broadcasted_iota(jnp.int32, (steps, positions), 0)
-    place = lax.broadcasted_iota(jnp.int32, (steps, positions), 1)
-    spread = jnp.where(place == length + step_of, 1.0, 0.0).astype(jnp.bfloat16)
-    fresh = lax.dot_general(
-        new_ref[0], spread, (((0,), (0,)), ((), ())), preferred_element_type=jnp.float32
-    )
+    owner = lax.broadcasted_iota(jnp.int32, (new_ref.shape[1], positions), 0)
+    place = lax.broadcasted_iota(jnp.int32, (new_ref.shape[1], positions), 1)
+    fresh = None
+    for s in range(steps):
+        spread = jnp.where((owner == r) & (place == length + s), 1.0, 0.0).astype(jnp.bfloat16)
+        piece = lax.dot_general(
+            new_ref[s], spread, (((0,), (0,)), ((), ())), preferred_element_type=jnp.float32
+        )
+        fresh = piece if fresh is None else fresh + piece
     column = lax.broadcasted_iota(jnp.int32, rows.shape, 1)
     is_new = (column >= length) & (column < length + steps)
     rows = jnp.where(is_new, fresh, rows.astype(jnp.float32)).astype(jnp.bfloat16)
@@ -371,7 +438,7 @@
         out_ref[s, 0] = attended[s * heads : (s + 1) * heads]
 
 
-def attend(me, slots_flat, move_key, cache_len, kv, arrivals, queries, new_latent):
+def attend(me, slot_table, move_key, cache_len, kv, arrivals, queries, new_latent):
     slots, width, positions = kv.shape
     steps, _, _, heads = queries.shape
     moves = arrivals.shape[0]
@@ -382,7 +449,7 @@
             pl.BlockSpec((1, width, positions), lambda r, *_: (r, 0, 0)),
             pl.BlockSpec((moves, width, positions), lambda r, *_: (0, 0, 0)),
             pl.BlockSpec((steps, 1, width, heads), lambda r, *_: (0, r, 0, 0)),
-            pl.BlockSpec((1, steps, width), lambda r, *_: (r, 0, 0)),
+            pl.BlockSpec(new_latent.shape, lambda r, *_: (0, 0, 0)),
         ],
         out_specs=[
             pl.BlockSpec((steps, 1, heads, LAT), lambda r, *_: (0, r, 0, 0)),
@@ -400,13 +467,13 @@
         name="attend",
     )(
         me,
-        slots_flat,
+        slot_table,
         move_key,
         cache_len,
         kv,
         arrivals,
         queries,
-        jnp.transpose(new_latent, (1, 0, 2)),
+        new_latent,
     )
 
 
@@ -425,14 +492,14 @@
     w_down,
 ):
     me = lax.axis_index("ep").reshape(1)
-    slots_flat = move_slot.reshape(-1)
+    slot_table = jnp.transpose(move_slot)
     kv = jnp.transpose(kv_cache, (0, 2, 1))
     moe_out, arrivals = layer(
-        slots_flat, move_key, kv, moe_in, expert_ids, expert_weights, w_gate, w_up, w_down
+        slot_table, move_key, kv, moe_in, expert_ids, expert_weights, w_gate, w_up, w_down
     )
     attention_out, cache = attend(
         me,
-        slots_flat,
+        slot_table,
         move_key,
         cache_len,
         kv,

time: 84.5 us -> 69.4 us (0.82)
  local copies, waits for them, and re-layouts: 8.08 us -> 0.65 us
  Pallas kernels: 72.7 us -> 67.9 us
  other arithmetic: 2.68 us -> 0 us
    pallas_call x1, Pallas kernels: 65.7 us -> 60.3 us  [layer(): pl.pallas_call(functools.partial(layer_kernel, groups, columns, orders),...]
    reshape x5 -> x0, local copies, waits for them, and re-layouts: 4.98 us -> none  [the longest x1 1.6 us: layer(): return (out.reshape(steps, token_count, width), arrivals)]
    unnamed x2 -> x0, other arithmetic: 2.68 us -> none
    unnamed x4 -> x3, local copies, waits for them, and re-layouts: 3.1 us -> 0.65 us
where the time goes in v1:
time: 69.4 us; the launch traced here: 69.2 us
  Pallas kernels  67.9 us (98%)
    pallas_call x1, Pallas kernels, layer(): pl.pallas_call(functools.partial(layer_kernel, groups, columns, orders),...  60.3 us
    pallas_call x1, Pallas kernels, attend(): pl.pallas_call(attend_kernel, grid_spec=grid, out_shape=[jax.ShapeDtypeSt...  7.58 us

profile of v1, /device:TPU:1, one launch (start us, length us, event | category | flops | bytes accessed | tf_op | source)
XLA Modules:
  0.0 69.2 jit_solution(10764910757266481783)
XLA Ops:
  0.6 60.3 %layer.1 = (bf16[2,4,7168]{2,1,0:T(4,128)(2,1)}, bf16[2,576,256]{2,1,0:T(8,128)(2,1)}) custom-call(s32[2,32]{1,0:T(2,128)} %bitcast.14, s32[2]{0:T(128)} %key_ref.1, s32[2,1,4]{2,1,0:T(1,128)} %bitcast.16, f32[2,1,4]{2,1,0:T(1,128)} %bitcast.17, bf16[4,576,256]{2,1,0:T(8,128)(2,1)} %bitcast.11, bf16[2,4,7168]{2,1,0:T(4,128)(2,1)} %refs_5_.1, ...), custom_call_target="tpu_custom_call" | custom-call | tf_op jit(solution)/shard_map/layer/pallas_call | solution.py:370
  60.9 0.0 copy-start
  60.9 7.6 %attend.1 = (bf16[2,4,128,512]{3,2,1,0:T(8,128)(2,1)}, bf16[4,576,256]{2,1,0:T(8,128)(2,1)}) custom-call(s32[1]{0:T(128)} %bitcast.me_ref, s32[2,32]{1,0:T(2,128)} %bitcast.15, s32[2]{0:T(128)} %key_ref.1, s32[128]{0:T(128)} %len_ref.1, bf16[4,576,256]{2,1,0:T(8,128)(2,1)} %bitcast.12, bf16[2,576,256]{2,1,0:T(8,128)(2,1)} %get-tuple-element.7.arr_ref, ...), custom_call_target="tpu_custom_call" | custom-call | tf_op jit(solution)/shard_map/attend/pallas_call | solution.py:459
  68.5 0.0 copy-done
  68.5 0.6 copy.18
Async XLA Ops:
  60.9 7.6 %copy-start = (bf16[2,4,7168]{2,1,0:T(4,128)(2,1)S(1)}, bf16[2,4,7168]{2,1,0:T(4,128)(2,1)}, u32[]{:S(2)}) copy-start(bf16[2,4,7168]{2,1,0:T(4,128)(2,1)} %get-tuple-element.16) | copy-start | bytes 344068

commit v2 on v1

--- a/solution.py
+++ b/solution.py
@@ -12,7 +12,6 @@
 MESH = pl.DeviceIdType.MESH
 LANES = 128
 ORDERS = ((3, 1, 2), (3, 2, 1)) * 3
-
 softmax_scale = 192.0 ** (-0.5)
 
 
@@ -43,6 +42,10 @@
         if mask >> bit & 1:
             slot |= 1 << place
     return slot
+
+
+def in_steps(parts, stages):
+    return [(p, stage) for stage in range(stages) for p in range(parts)]
 
 
 def layer_kernel(groups, columns, orders, *refs):
@@ -192,31 +195,26 @@
 
     across = [[] for _ in range(parts)]
     link = [None] * parts
-    for p, place in enumerate(place_of):
-        mine = pack(0, *place)
-        for copy in first[p]:
-            copy.wait_recv()
-        pieces = [mine]
-        pieces += [arrive[p][d].astype(jnp.float32) for d in range(1, groups)]
-        held[p][0] = jnp.concatenate(pieces, axis=0).astype(jnp.bfloat16)
-        link[p] = send(held[p].at[0:1], held[p].at[1:2], 1 << ORDERS[p][0])
-        across[p].append(send(held[p].at[0:1], held[p].at[8:9], 1))
-        everything += first[p]
-    for stage in range(3):
-        have = 1 << stage
-        for p in range(parts):
+    for p, stage in in_steps(parts, 4):
+        if stage == 0:
+            mine = pack(0, *place_of[p])
+            for copy in first[p]:
+                copy.wait_recv()
+            everything += first[p]
+            pieces = [mine]
+            pieces += [arrive[p][d].astype(jnp.float32) for d in range(1, groups)]
+            held[p][0] = jnp.concatenate(pieces, axis=0).astype(jnp.bfloat16)
+        else:
             link[p].wait_recv()
             everything.append(link[p])
-            if stage < 2:
-                link[p] = send(
-                    held[p].at[0 : 2 * have],
-                    held[p].at[2 * have : 4 * have],
-                    1 << ORDERS[p][stage + 1],
-                )
-            across[p].append(
-                send(held[p].at[have : 2 * have], held[p].at[8 + have : 8 + 2 * have], 1)
+        have = 1 << stage
+        if stage < 3:
+            link[p] = send(
+                held[p].at[0:have], held[p].at[have : 2 * have], 1 << ORDERS[p][stage]
             )
-        if stage == 0:
+        low = have // 2
+        across[p].append(send(held[p].at[low:have], held[p].at[8 + low : 8 + have], 1))
+        if (p, stage) == (parts - 1, 1):
             advance()
 
     loads[0].wait()
@@ -269,45 +267,38 @@
                     across[p].append(send(sums[p].at[a:b], taken[p].at[a:b], 1))
 
     def add(p, low, high, shift):
-        total = sums[p][low:high].astype(jnp.float32)
-        total += taken[p][low + shift : high + shift].astype(jnp.float32)
-        sums[p][low:high] = total.astype(jnp.bfloat16)
-
-    for p in range(parts):
-        across[p][0].wait_recv()
-        add(p, 4, 8, 8)
-        link[p] = send(sums[p].at[4:8], taken[p].at[4:8], 1 << ORDERS[p][2])
-    for p in range(parts):
-        across[p][1].wait_recv()
-        across[p][2].wait_recv()
-        everything += across[p]
-        add(p, 0, 4, 8)
-    advance()
-    for stage in (1, 0):
-        have = 1 << stage
-        for p in range(parts):
+        sums[p][low:high] = sums[p][low:high] + taken[p][low + shift : high + shift]
+
+    last = [None] * parts
+    for p, stage in in_steps(parts, 4):
+        if stage == 0:
+            across[p][0].wait_recv()
+            add(p, 4, 8, 8)
+            link[p] = send(sums[p].at[4:8], taken[p].at[4:8], 1 << ORDERS[p][2])
+            across[p][1].wait_recv()
+            across[p][2].wait_recv()
+            everything += across[p]
+            add(p, 0, 4, 8)
+        elif stage < 3:
+            have = 4 >> stage
             link[p].wait_recv()
             everything.append(link[p])
             add(p, have, 2 * have, 2 * have)
             link[p] = send(
-                sums[p].at[have : 2 * have], taken[p].at[have : 2 * have], 1 << ORDERS[p][stage]
+                sums[p].at[have : 2 * have],
+                taken[p].at[have : 2 * have],
+                1 << ORDERS[p][2 - stage],
             )
-        for p in range(parts):
             add(p, 0, have, 2 * have)
-        if stage == 1:
+        else:
+            link[p].wait_recv()
+            everything.append(link[p])
+            total = sums[p][0].astype(jnp.float32) + taken[p][1].astype(jnp.float32)
+            for d in range(groups):
+                final[p][d] = total[d * token_rows : (d + 1) * token_rows].astype(jnp.bfloat16)
+            last[p] = [send(final[p].at[d], ended[p].at[d], SPLIT * d) for d in range(1, groups)]
+        if p == parts - 1 and stage != 2:
             advance()
-
-    last = []
-    for p in range(parts):
-        link[p].wait_recv()
-        everything.append(link[p])
-        total = sums[p][0].astype(jnp.float32) + taken[p][1].astype(jnp.float32)
-        for d in range(groups):
-            final[p][d] = total[d * token_rows : (d + 1) * token_rows].astype(jnp.bfloat16)
-        last.append(
-            [send(final[p].at[d], ended[p].at[d], SPLIT * d) for d in range(1, groups)]
-        )
-    advance()
     row_of = lax.broadcasted_iota(jnp.int32, (token_rows, LANES), 0)
     gains = []
     for d in range(groups):
@@ -397,63 +388,72 @@
 def attend_kernel(
     me_ref, slot_ref, key_ref, len_ref, kv_ref, arr_ref, q_ref, new_ref, out_ref, cache_ref
 ):
-    r = pl.program_id(0)
-    me, slots, moves = me_ref[0], pl.num_programs(0), arr_ref.shape[0]
-    length = len_ref[me * slots + r]
-    rows = kv_ref[0]
-    for k in range(moves):
-        here = slot_ref[k, me] == r
-        partner = me ^ key_ref[k]
-        length = jnp.where(here, len_ref[partner * slots + slot_ref[k, partner]], length)
-        rows = jnp.where(here, arr_ref[k], rows)
+    me, moves = me_ref[0], arr_ref.shape[0]
+    together = kv_ref.shape[0]
+    slots = pl.num_programs(0) * together
     steps, heads = q_ref.shape[0], q_ref.shape[3]
-    positions = rows.shape[1]
+    positions = kv_ref.shape[2]
     owner = lax.broadcasted_iota(jnp.int32, (new_ref.shape[1], positions), 0)
     place = lax.broadcasted_iota(jnp.int32, (new_ref.shape[1], positions), 1)
-    fresh = None
-    for s in range(steps):
-        spread = jnp.where((owner == r) & (place == length + s), 1.0, 0.0).astype(jnp.bfloat16)
-        piece = lax.dot_general(
-            new_ref[s], spread, (((0,), (0,)), ((), ())), preferred_element_type=jnp.float32
+    at = lax.broadcasted_iota(jnp.int32, (steps * heads, positions), 1)
+    step = lax.broadcasted_iota(jnp.int32, (steps * heads, positions), 0) // heads
+    column = lax.broadcasted_iota(jnp.int32, (1, positions), 1)
+    for n in range(together):
+        r = pl.program_id(0) * together + n
+        length = len_ref[me * slots + r]
+        rows = kv_ref[n]
+        for k in range(moves):
+            here = slot_ref[k, me] == r
+            partner = me ^ key_ref[k]
+            length = jnp.where(here, len_ref[partner * slots + slot_ref[k, partner]], length)
+            rows = jnp.where(here, arr_ref[k], rows)
+        fresh = None
+        for s in range(steps):
+            spread = jnp.where((owner == r) & (place == length + s), 1.0, 0.0).astype(jnp.bfloat16)
+            piece = lax.dot_general(
+                new_ref[s], spread, (((0,), (0,)), ((), ())), preferred_element_type=jnp.float32
+            )
+            fresh = piece if fresh is None else fresh + piece
+        keep = jnp.where((column >= length) & (column < length + steps), 0.0, 1.0)
+        rows = rows * keep.astype(jnp.bfloat16) + fresh.astype(jnp.bfloat16)
+        cache_ref[n] = rows
+        merged = jnp.concatenate([q_ref[s, n] for s in range(steps)], axis=1)
+        scores = (
+            lax.dot_general(
+                merged, rows, (((0,), (0,)), ((), ())), preferred_element_type=jnp.float32
+            )
+            * softmax_scale
         )
-        fresh = piece if fresh is None else fresh + piece
-    column = lax.broadcasted_iota(jnp.int32, rows.shape, 1)
-    is_new = (column >= length) & (column < length + steps)
-    rows = jnp.where(is_new, fresh, rows.astype(jnp.float32)).astype(jnp.bfloat16)
-    cache_ref[0] = rows
-    merged = jnp.concatenate([q_ref[s, 0] for s in range(steps)], axis=1)
-    scores = (
-        lax.dot_general(merged, rows, (((0,), (0,)), ((), ())), preferred_element_type=jnp.float32)
-        * softmax_scale
-    )
-    at = lax.broadcasted_iota(jnp.int32, scores.shape, 1)
-    step = lax.broadcasted_iota(jnp.int32, scores.shape, 0) // heads
-    scores = jnp.where(at < length + step + 1, scores, jnp.float32(-1e30))
-    weights = jnp.exp(scores - jnp.max(scores, axis=-1, keepdims=True))
-    probabilities = (weights / jnp.sum(weights, axis=-1, keepdims=True)).astype(jnp.bfloat16)
-    attended = lax.dot_general(
-        probabilities, rows[:LAT], (((1,), (1,)), ((), ())), preferred_element_type=jnp.float32
-    ).astype(jnp.bfloat16)
-    for s in range(steps):
-        out_ref[s, 0] = attended[s * heads : (s + 1) * heads]
+        scores = jnp.where(at < length + step + 1, scores, jnp.float32(-1e30))
+        weights = jnp.exp(scores - jnp.max(scores, axis=-1, keepdims=True))
+        inverse = 1.0 / jnp.sum(weights, axis=-1, keepdims=True)
+        attended = lax.dot_general(
+            (weights * inverse).astype(jnp.bfloat16),
+            rows[:LAT],
+            (((1,), (1,)), ((), ())),
+            preferred_element_type=jnp.float32,
+        ).astype(jnp.bfloat16)
+        for s in range(steps):
+            out_ref[s, n] = attended[s * heads : (s + 1) * heads]
 
 
 def attend(me, slot_table, move_key, cache_len, kv, arrivals, queries, new_latent):
     slots, width, positions = kv.shape
     steps, _, _, heads = queries.shape
     moves = arrivals.shape[0]
+    together = 2
     grid = pltpu.PrefetchScalarGridSpec(
         num_scalar_prefetch=4,
-        grid=(slots,),
+        grid=(slots // together,),
         in_specs=[
-            pl.BlockSpec((1, width, positions), lambda r, *_: (r, 0, 0)),
+            pl.BlockSpec((together, width, positions), lambda r, *_: (r, 0, 0)),
             pl.BlockSpec((moves, width, positions), lambda r, *_: (0, 0, 0)),
-            pl.BlockSpec((steps, 1, width, heads), lambda r, *_: (0, r, 0, 0)),
+            pl.BlockSpec((steps, together, width, heads), lambda r, *_: (0, r, 0, 0)),
             pl.BlockSpec(new_latent.shape, lambda r, *_: (0, 0, 0)),
         ],
         out_specs=[
-            pl.BlockSpec((steps, 1, heads, LAT), lambda r, *_: (0, r, 0, 0)),
-            pl.BlockSpec((1, width, positions), lambda r, *_: (r, 0, 0)),
+            pl.BlockSpec((steps, together, heads, LAT), lambda r, *_: (0, r, 0, 0)),
+            pl.BlockSpec((together, width, positions), lambda r, *_: (r, 0, 0)),
         ],
     )
     return pl.pallas_call(

time: 69.4 us -> 68.3 us (0.984)
  Pallas kernels: 67.9 us -> 66.9 us
    pallas_call x1, Pallas kernels: 7.58 us -> 6.62 us  [attend(): pl.pallas_call(attend_kernel, grid_spec=grid, out_shape=[jax.ShapeDtypeSt...]
where the time goes in v2:
time: 68.3 us; the launch traced here: 68.2 us
  Pallas kernels  66.9 us (98%)
    pallas_call x1, Pallas kernels, layer(): pl.pallas_call(functools.partial(layer_kernel, groups, columns, orders),...  60.2 us
    pallas_call x1, Pallas kernels, attend(): pl.pallas_call(attend_kernel, grid_spec=grid, out_shape=[jax.ShapeDtypeSt...  6.62 us

profile of v2, /device:TPU:1, one launch (start us, length us, event | category | flops | bytes accessed | tf_op | source)
XLA Modules:
  0.0 68.2 jit_solution(11591210232809207853)
XLA Ops:
  0.6 60.2 %layer.1 = (bf16[2,4,7168]{2,1,0:T(4,128)(2,1)}, bf16[2,576,256]{2,1,0:T(8,128)(2,1)}) custom-call(s32[2,32]{1,0:T(2,128)} %bitcast.14, s32[2]{0:T(128)} %key_ref.1, s32[2,1,4]{2,1,0:T(1,128)} %bitcast.16, f32[2,1,4]{2,1,0:T(1,128)} %bitcast.17, bf16[4,576,256]{2,1,0:T(8,128)(2,1)} %bitcast.11, bf16[2,4,7168]{2,1,0:T(4,128)(2,1)} %refs_5_.1, ...), custom_call_target="tpu_custom_call" | custom-call | tf_op jit(solution)/shard_map/layer/pallas_call | solution.py:361
  60.9 0.0 copy-start
  60.9 6.6 %attend.1 = (bf16[2,4,128,512]{3,2,1,0:T(8,128)(2,1)}, bf16[4,576,256]{2,1,0:T(8,128)(2,1)}) custom-call(s32[1]{0:T(128)} %bitcast.me_ref, s32[2,32]{1,0:T(2,128)} %bitcast.15, s32[2]{0:T(128)} %key_ref.1, s32[128]{0:T(128)} %len_ref.1, bf16[4,576,256]{2,1,0:T(8,128)(2,1)} %bitcast.12, bf16[2,576,256]{2,1,0:T(8,128)(2,1)} %get-tuple-element.7.arr_ref, ...), custom_call_target="tpu_custom_call" | custom-call | tf_op jit(solution)/shard_map/attend/pallas_call | solution.py:459
  67.5 0.0 copy-done
  67.5 0.6 copy.18
Async XLA Ops:
  60.9 6.6 %copy-start = (bf16[2,4,7168]{2,1,0:T(4,128)(2,1)S(1)}, bf16[2,4,7168]{2,1,0:T(4,128)(2,1)}, u32[]{:S(2)}) copy-start(bf16[2,4,7168]{2,1,0:T(4,128)(2,1)} %get-tuple-element.16) | copy-start | bytes 344068
